TPU v7x, 32 devices: a whole 2x2x4 slice. The times are simulated.
32 devices in a mesh: groups: 2 (over x), frame: 16 (over z, y, core).
Axes of the slice: x: 2, y: 2, z: 4, core: 2. Of those that a mesh axis runs over, the one named last changes fastest.
Arguments:
- lowres: bfloat16 [32, 64, 128], P(('groups', 'frame')), parts along dimension 0, may hold values from -6 to 6
- noisy: bfloat16 [32, 8, 64, 128], P(('groups', 'frame')), parts along dimension 0, may hold values from -6 to 6
- starts: int32 [8], P('groups'), parts along dimension 0, may hold values from 0 to 8, as said below
- blend: int32 [8, 8], P('groups'), parts along dimension 0, may hold values from 1 to 4
- assign: int32 [32], P('groups'), parts along dimension 0, may hold values from 0 to 15, each once
- base_w: bfloat16 [3, 128, 128], replicated, may hold values from -0.3125 to 0.3125
- cond_w: bfloat16 [128, 128], replicated, may hold values from -0.5 to 0.5
- noise_w: bfloat16 [128, 128], replicated, may hold values from -0.5 to 0.5
- gains: float32 [3, 128], replicated, may hold values from 0.25 to 1.75
- tconv: float32 [3, 3, 128], replicated, may hold values from -3 to 3
- mlp_in: bfloat16 [3, 128, 512], replicated, may hold values from -0.5 to 0.5
- mlp_out: bfloat16 [3, 512, 128], replicated, may hold values from -0.25 to 0.25
Outputs:
- video: bfloat16 [32, 256, 128], P(('groups', 'frame')), parts along dimension 0
There are 2 independent parts, one for each index of `groups`. A program takes and returns all parts, laid end to end along the dimension named above; an argument that names none is the same for every part. Nothing has to cross between parts.
Inputs may be any that keep to these rules, and one draw needn't show every extreme that they name: Window k covers frames starts[k] to starts[k] + 7; every frame lies in some window; the first window starts at 0 and the last at 8.
All inputs are finite; a program needn't handle non-finite values.
Results may differ from a plain program's by a relative error of at most 0.0059.
Values may be sent and summed in bfloat16 or wider, within the bound.
A program may use at most 64 MiB of HBM per device.

v0:
```python
import jax
import jax.numpy as jnp
from jax import lax
from jax.sharding import PartitionSpec as P

TILES = 4


def padded_2(cells, sides, width):
    for axis, dim in sides:
        count = lax.axis_size(axis)
        ends = count - 1
        head = lax.slice_in_dim(cells, 0, width, axis=dim)
        tail = lax.slice_in_dim(cells, cells.shape[dim] - width, cells.shape[dim], axis=dim)
        cells = jnp.concatenate(
            [
                lax.ppermute(tail, axis, [(i, (i + 1) % count) for i in range(ends)]),
                cells,
                lax.ppermute(head, axis, [((i + 1) % count, i) for i in range(ends)]),
            ],
            axis=dim,
        )
    return cells


def refine_block(cond, noisy_item, cond_w, noise_w, gains, tconv, mlp_in, mlp_out):
    frame_count, positions, channels = cond.shape
    row_count = frame_count * positions
    state = jnp.dot(cond.reshape(row_count, channels), cond_w, preferred_element_type=jnp.float32)
    state = state + jnp.dot(
        noisy_item.reshape(row_count, channels), noise_w, preferred_element_type=jnp.float32
    )
    for layer_id in range(gains.shape[0]):
        inverse = lax.rsqrt(jnp.mean(state * state, axis=-1, keepdims=True) + 1e-06)
        normed = (state * inverse * gains[layer_id]).reshape(frame_count, positions, channels)
        zeros_frame = jnp.zeros_like(normed[:1])
        before = jnp.concatenate([zeros_frame, normed[:-1]], 0)
        behind = jnp.concatenate([normed[1:], zeros_frame], 0)
        mixed_rows = (
            normed
            + tconv[layer_id, 0] * before
            + tconv[layer_id, 1] * normed
            + tconv[layer_id, 2] * behind
        )
        mixed_rows = mixed_rows.reshape(row_count, channels).astype(jnp.bfloat16)
        hidden = jax.nn.silu(
            jnp.dot(mixed_rows, mlp_in[layer_id], preferred_element_type=jnp.float32)
        ).astype(jnp.bfloat16)
        state = state + jnp.dot(hidden, mlp_out[layer_id], preferred_element_type=jnp.float32)
    return state.astype(jnp.bfloat16).reshape(frame_count, positions, channels)


def refine(cond, noisy_item, cond_w, noise_w, gains, tconv, mlp_in, mlp_out):
    frame_count, positions, channels = cond.shape
    block_count = positions // positions
    cond_blocks = jnp.transpose(
        cond.reshape(frame_count, block_count, positions, channels), (1, 0, 2, 3)
    )
    noisy_blocks = jnp.transpose(
        noisy_item.reshape(frame_count, block_count, positions, channels), (1, 0, 2, 3)
    )

    def one_block(pair):
        return refine_block(pair[0], pair[1], cond_w, noise_w, gains, tconv, mlp_in, mlp_out)

    outputs = lax.map(one_block, (cond_blocks, noisy_blocks))
    return jnp.transpose(outputs, (1, 0, 2, 3)).reshape(frame_count, positions, channels)


def on_device(
    lowres, noisy, starts, blend, assign, base_w, cond_w, noise_w, gains, tconv, mlp_in, mlp_out
):
    frame_total = assign.shape[0]
    window_len = noisy.shape[1]
    tile_pos = noisy.shape[2]
    channels = noisy.shape[3]
    low_pos = lowres.shape[1] // TILES
    padded = padded_2(lowres, (("frame", 0),), 1)
    total = jnp.dot(padded[0], base_w[0], preferred_element_type=jnp.float32)
    total = total + jnp.dot(padded[1], base_w[1], preferred_element_type=jnp.float32)
    total = total + jnp.dot(padded[2], base_w[2], preferred_element_type=jnp.float32)
    base_frame = (lowres[0].astype(jnp.float32) + jax.nn.silu(total)).astype(jnp.bfloat16)
    own_index = lax.axis_index("frame")
    item_id = assign[own_index]
    own_start = starts[item_id // TILES]
    tile_rows = base_frame.reshape(TILES, low_pos * channels)
    picker = (assign[:, None] % TILES == jnp.arange(TILES, dtype=jnp.int32)[None, :]).astype(
        jnp.bfloat16
    )
    outgoing = jnp.dot(picker, tile_rows, preferred_element_type=jnp.float32).astype(jnp.bfloat16)
    outgoing = outgoing.reshape(frame_total, low_pos, channels)
    gathered = lax.all_to_all(outgoing, "frame", split_axis=0, concat_axis=0, tiled=True)
    window_tiles = lax.dynamic_slice_in_dim(gathered, own_start, window_len, 0)
    cond = jnp.repeat(window_tiles, 4, axis=1)
    refined = refine(cond, noisy[0], cond_w, noise_w, gains, tconv, mlp_in, mlp_out)
    source_window = assign // TILES
    source_tile = assign % TILES
    placed = jnp.zeros((frame_total, tile_pos, channels), jnp.bfloat16)
    placed = lax.dynamic_update_slice_in_dim(placed, refined, own_start, 0)
    received = lax.all_to_all(placed, "frame", split_axis=0, concat_axis=0, tiled=True)
    offset = own_index - starts[source_window]
    inside = (offset >= 0) & (offset < window_len)
    clipped = jnp.clip(offset, 0, window_len - 1)
    factor = jnp.where(inside, blend[source_window, clipped], 0).astype(jnp.float32)
    tile_match = (source_tile[None, :] == jnp.arange(TILES, dtype=jnp.int32)[:, None]).astype(
        jnp.float32
    )
    blend_matrix = tile_match * factor[None, :]
    weighted = jnp.dot(
        blend_matrix.astype(jnp.bfloat16),
        received.reshape(frame_total, tile_pos * channels),
        preferred_element_type=jnp.float32,
    )
    denom = jnp.sum(blend_matrix, axis=1)
    video = weighted / denom[:, None]
    return video.reshape(1, TILES * tile_pos, channels).astype(jnp.bfloat16)


def solution(mesh):
    in_specs = (
        P(("groups", "frame"), None, None),
        P(("groups", "frame"), None, None, None),
        P("groups"),
        P("groups", None),
        P("groups"),
        P(),
        P(),
        P(),
        P(),
        P(),
        P(),
        P(),
    )
    out_specs = P(("groups", "frame"), None, None)
    return jax.shard_map(
        on_device, mesh=mesh, in_specs=in_specs, out_specs=out_specs, check_vma=False
    )
```

profile of v0, /device:TPU:0, one launch (start us, length us, event | category | flops | bytes accessed | tf_op | source)
XLA Modules:
  0.0 52.0 jit_solution(3728004417824354756)
XLA Ops:
  0.0 1.4 %collective-permute-start.1 = (bf16[1,64,128]{2,1,0:T(8,128)(2,1)}, bf16[1,64,128]{2,1,0:T(8,128)(2,1)S(1)}, u32[]{:S(2)}, u32[]{:S(2)}) collective-permute-start(bf16[1,64,128]{2,1,0:T(8,128)(2,1)} %param.12), channel_id=1, source_target_pairs={{1,0},{2,1},{3,2},{4,3},{5,4},{6,5},{7,6},{8,7},{9,8},{10,9},{11,1... | collective-permute-start | bytes 49160 | tf_op jit(solution)/shard_map/ppermute | solution.py:19
  1.4 3.0 %collective-permute-start = (bf16[1,64,128]{2,1,0:T(8,128)(2,1)}, bf16[1,64,128]{2,1,0:T(8,128)(2,1)S(1)}, u32[]{:S(2)}, u32[]{:S(2)}) collective-permute-start(bf16[1,64,128]{2,1,0:T(8,128)(2,1)} %param.12), channel_id=1, source_target_pairs={{0,1},{1,2},{2,3},{3,4},{4,5},{5,6},{6,7},{7,8},{8,9},{9,10},{10,1... | collective-permute-start | bytes 49160 | tf_op jit(solution)/shard_map/ppermute | solution.py:17
  4.5 0.7 %compare_select_fusion.1 = (s32[16]{0:T(128)S(1)}, s32[16]{0:T(128)S(1)}) fusion(s32[16]{0:T(128)} %param.16), kind=kLoop, calls=%fused_computation.58 | loop fusion | flops 352 | bytes 192 | tf_op jit(solution)/shard_map/select_n | solution.py:101
  5.1 0.9 %fusion.29 = f32[64,128]{1,0:T(8,128)S(1)} fusion(bf16[3,128,128]{2,1,0:T(8,128)(2,1)} %param.17, bf16[1,64,128]{2,1,0:T(8,128)(2,1)} %param.12), kind=kOutput, calls=%fused_computation.44 | convolution fusion | flops 2097152 | bytes 81920 | tf_op jit(solution)/shard_map/dot_general | solution.py:80
  6.1 0.6 %copy-done.11 = s32[16]{0:T(128)S(1)} copy-done((s32[16]{0:T(128)S(1)}, s32[16]{0:T(128)}, u32[]{:S(2)}) %copy-start.11) | copy-done | bytes 88
  6.7 0.6 %dynamic_slice.14 = s32[1]{0:T(128)} dynamic-slice(s32[16]{0:T(128)S(1)} %copy-done.11, s32[]{:T(128)S(6)} %select_n.58), dynamic_slice_sizes={1} | dynamic-slice | bytes 12 | tf_op jit(solution)/shard_map/dynamic_slice | solution.py:84
  9.9 0.6 %copy-done.1 = s32[4]{0:T(128)S(1)} copy-done((s32[4]{0:T(128)S(1)}, s32[4]{0:T(128)}, u32[]{:S(2)}) %copy-start.1) | copy-done | bytes 40
  10.6 0.6 %dynamic_slice.15 = s32[1]{0:T(128)} dynamic-slice(s32[4]{0:T(128)S(1)} %copy-done.1, s32[]{:T(128)S(6)} %select_n.60), dynamic_slice_sizes={1} | dynamic-slice | bytes 12 | tf_op jit(solution)/shard_map/dynamic_slice | solution.py:85
  12.5 0.7 %gather_fusion = s32[16]{0:T(128)S(1)} fusion(s32[4]{0:T(128)S(1)} %copy-done.1, s32[1024]{0:T(1024)S(1)} %pad_clamp_fusion), kind=kCustom, calls=%fused_computation | custom fusion | bytes 192 | tf_op jit(solution)/shard_map/gather | solution.py:101
  14.0 0.6 %copy-done.6 = bf16[1,64,128]{2,1,0:T(8,128)(2,1)S(1)} copy-done((bf16[1,64,128]{2,1,0:T(8,128)(2,1)S(1)}, bf16[1,64,128]{2,1,0:T(8,128)(2,1)}, u32[]{:S(2)}) %copy-start.6) | copy-done | bytes 16408
  14.5 0.1 add_convert_fusion.3
  14.7 0.2 fusion.2
  14.9 0.6 %copy.13 = bf16[2,8,16,128]{3,2,1,0:T(8,128)(2,1)} copy(bf16[2,8,16,128]{3,1,2,0:T(8,128)(2,1)S(1)} %fusion.2) | data formatting | bytes 131072
  15.6 8.1 %all-to-all-start = ((bf16[16,16,128]{2,1,0:T(8,128)(2,1)}), bf16[16,16,128]{2,1,0:T(8,128)(2,1)S(1)}, u32[]{:S(2)}, u32[]{:S(2)}) async-start(bf16[16,16,128]{2,1,0:T(8,128)(2,1)} %bitcast.45), calls=%async_computation | async-start | bytes 131072 | tf_op jit(solution)/shard_map/all_to_all | solution.py:92
  23.7 6.9 %all-to-all-done = bf16[16,16,128]{2,1,0:T(8,128)(2,1)S(1)} async-done(((bf16[16,16,128]{2,1,0:T(8,128)(2,1)}), bf16[16,16,128]{2,1,0:T(8,128)(2,1)S(1)}, u32[]{:S(2)}, u32[]{:S(2)}) %all-to-all-start) | async-done | bytes 65568 | tf_op jit(solution)/shard_map/all_to_all | solution.py:92
  30.6 0.7 %copy-done.4 = bf16[128,128]{1,0:T(8,128)(2,1)S(1)} copy-done((bf16[128,128]{1,0:T(8,128)(2,1)S(1)}, bf16[128,128]{1,0:T(8,128)(2,1)}, u32[]{:S(2)}) %copy-start.4) | copy-done | bytes 32792
  31.3 0.2 fusion.60
  31.5 0.6 %copy-done.5 = bf16[128,128]{1,0:T(8,128)(2,1)S(1)} copy-done((bf16[128,128]{1,0:T(8,128)(2,1)S(1)}, bf16[128,128]{1,0:T(8,128)(2,1)}, u32[]{:S(2)}) %copy-start.5) | copy-done | bytes 32792
  32.1 0.3 multiply_reduce_fusion.2
  32.4 0.1 multiply_multiply_fusion.2
  32.7 0.9 %copy-done.9 = bf16[3,512,128]{2,1,0:T(8,128)(2,1)S(1)} copy-done((bf16[3,512,128]{2,1,0:T(8,128)(2,1)S(1)}, bf16[3,512,128]{2,1,0:T(8,128)(2,1)}, u32[]{:S(2)}) %copy-start.9) | copy-done | bytes 393240
  33.7 0.6 %multiply_reduce_fusion.1 = (f32[512]{0:T(512)S(1)}, f32[512,128]{1,0:T(8,128)S(1)}) fusion(f32[512,128]{1,0:T(8,128)S(1)} %get-tuple-element.56, bf16[3,512,128]{2,1,0:T(8,128)(2,1)S(1)} %copy-done.9, bf16[512,128]{1,0:T(8,128)(2,1)S(1)} %bitcast.129, bf16[3,128,512]{2,1,0:T(8,128)(2,1)S(1)} %copy-done.10), kind=kOutput, calls=%fused_computation.26 | convolution fusion | flops 135724544 | bytes 919552 | tf_op jit(solution)/shard_map/while/body/eval_jaxpr/dot_general | solution.py:49
  34.6 0.6 %multiply_reduce_fusion = (f32[512]{0:T(512)S(1)}, f32[512,128]{1,0:T(8,128)S(1)}) fusion(f32[512,128]{1,0:T(8,128)S(1)} %get-tuple-element.58, bf16[3,512,128]{2,1,0:T(8,128)(2,1)S(1)} %copy-done.9, bf16[512,128]{1,0:T(8,128)(2,1)S(1)} %bitcast.130, bf16[3,128,512]{2,1,0:T(8,128)(2,1)S(1)} %copy-done.10), kind=kOutput, calls=%fused_computation.23 | convolution fusion | flops 135724544 | bytes 919552 | tf_op jit(solution)/shard_map/while/body/eval_jaxpr/dot_general | solution.py:49
  35.5 0.6 %fusion.1 = bf16[512,128]{1,0:T(8,128)(2,1)S(1)} fusion(f32[512,128]{1,0:T(8,128)S(1)} %get-tuple-element.60, bf16[512,128]{1,0:T(8,128)(2,1)S(1)} %bitcast.131, bf16[3,512,128]{2,1,0:T(8,128)(2,1)S(1)} %copy-done.9, bf16[3,128,512]{2,1,0:T(8,128)(2,1)S(1)} %copy-done.10), kind=kOutput, calls=%fused_computation.9 | convolution fusion | flops 135659520 | bytes 786432 | tf_op jit(solution)/shard_map/while/body/eval_jaxpr/dot_general | solution.py:49
  36.1 0.8 %broadcast_in_dim.18 = bf16[16,64,128]{2,1,0:T(8,128)(2,1)} broadcast(bf16[]{:T(256)} %constant.86.clone.1), dimensions={} | broadcast | bytes 262146 | tf_op jit(solution)/shard_map/broadcast_in_dim | solution.py:98
  36.8 0.7 %constant_dynamic-update-slice_fusion = bf16[16,64,128]{2,1,0:T(8,128)(2,1)} fusion(bf16[16,64,128]{2,1,0:T(8,128)(2,1)} %broadcast_in_dim.18, bf16[8,64,128]{2,1,0:T(8,128)(2,1)S(1)} %bitcast.128, s32[]{:T(128)S(6)} %select_n.61), kind=kLoop, calls=%fused_computation.89 | loop fusion | bytes 262148 | tf_op jit(solution)/shard_map/dynamic_update_slice | solution.py:99
  37.5 3.5 %all-to-all-start.1 = ((bf16[16,64,128]{2,1,0:T(8,128)(2,1)}), bf16[16,64,128]{2,1,0:T(8,128)(2,1)S(1)}, u32[]{:S(2)}, u32[]{:S(2)}) async-start(bf16[16,64,128]{2,1,0:T(8,128)(2,1)} %constant_dynamic-update-slice_fusion), calls=%async_computation.1 | async-start | bytes 524288 | tf_op jit(solution)/shard_map/all_to_all | solution.py:100
  41.1 0.7 %copy-done.2 = s32[4,8]{1,0:T(4,128)S(1)} copy-done((s32[4,8]{1,0:T(4,128)S(1)}, s32[4,8]{1,0:T(4,128)}, u32[]{:S(2)}) %copy-start.2) | copy-done | bytes 152
  41.7 0.7 %gather_fusion.1 = s32[16]{0:T(128)S(1)} fusion(s32[4,8]{1,0:T(4,128)S(1)} %copy-done.2, s32[16]{0:T(128)S(1)} %fusion.47), kind=kCustom, calls=%fused_computation.1 | custom fusion | bytes 256 | tf_op jit(solution)/shard_map/gather | solution.py:104
  42.5 8.5 %all-to-all-done.1 = bf16[16,64,128]{2,1,0:T(8,128)(2,1)S(1)} async-done(((bf16[16,64,128]{2,1,0:T(8,128)(2,1)}), bf16[16,64,128]{2,1,0:T(8,128)(2,1)S(1)}, u32[]{:S(2)}, u32[]{:S(2)}) %all-to-all-start.1) | async-done | bytes 262176 | tf_op jit(solution)/shard_map/all_to_all | solution.py:100
  51.1 0.3 fusion
  51.3 0.7 %convert_element_type.88 = bf16[1,256,128]{2,1,0:T(8,128)(2,1)} reshape(bf16[4,8192]{1,0:T(4,128)(2,1)S(1)} %fusion) | data formatting | bytes 131072 | tf_op jit(solution)/shard_map/convert_element_type | solution.py:116
  (40 shorter events, 1.1 us)
Async XLA Ops:
  0.0 31.5 %copy-start = (bf16[1,8,64,128]{3,2,1,0:T(8,128)(2,1)S(1)}, bf16[1,8,64,128]{3,2,1,0:T(8,128)(2,1)}, u32[]{:S(2)}) copy-start(bf16[1,8,64,128]{3,2,1,0:T(8,128)(2,1)} %param.13) | copy-start | bytes 393220
  0.0 13.8 %collective-permute-start.1 = (bf16[1,64,128]{2,1,0:T(8,128)(2,1)}, bf16[1,64,128]{2,1,0:T(8,128)(2,1)S(1)}, u32[]{:S(2)}, u32[]{:S(2)}) collective-permute-start(bf16[1,64,128]{2,1,0:T(8,128)(2,1)} %param.12), channel_id=1, source_target_pairs={{1,0},{2,1},{3,2},{4,3},{5,4},{6,5},{7,6},{8,7},{9,8},{10,9},{11,1... | collective-permute-start | bytes 49160 | tf_op jit(solution)/shard_map/ppermute | solution.py:19
  1.4 12.5 %collective-permute-start = (bf16[1,64,128]{2,1,0:T(8,128)(2,1)}, bf16[1,64,128]{2,1,0:T(8,128)(2,1)S(1)}, u32[]{:S(2)}, u32[]{:S(2)}) collective-permute-start(bf16[1,64,128]{2,1,0:T(8,128)(2,1)} %param.12), channel_id=1, source_target_pairs={{0,1},{1,2},{2,3},{3,4},{4,5},{5,6},{6,7},{7,8},{8,9},{9,10},{10,1... | collective-permute-start | bytes 49160 | tf_op jit(solution)/shard_map/ppermute | solution.py:17
  5.1 0.9 %copy-start.7 = (f32[3,3,128]{2,1,0:T(4,128)S(1)}, f32[3,3,128]{2,1,0:T(4,128)}, u32[]{:S(2)}) copy-start(f32[3,3,128]{2,1,0:T(4,128)} %param.21) | copy-start | bytes 13828
  6.1 0.7 %copy-start.11 = (s32[16]{0:T(128)S(1)}, s32[16]{0:T(128)}, u32[]{:S(2)}) copy-start(s32[16]{0:T(128)} %param.16) | copy-start | bytes 196
  9.9 0.7 %copy-start.1 = (s32[4]{0:T(128)S(1)}, s32[4]{0:T(128)}, u32[]{:S(2)}) copy-start(s32[4]{0:T(128)} %param.14) | copy-start | bytes 52
  12.5 1.4 %copy-start.3 = (bf16[3,128,128]{2,1,0:T(8,128)(2,1)S(1)}, bf16[3,128,128]{2,1,0:T(8,128)(2,1)}, u32[]{:S(2)}) copy-start(bf16[3,128,128]{2,1,0:T(8,128)(2,1)} %param.17) | copy-start | bytes 294916
  13.8 0.7 %copy-start.6 = (bf16[1,64,128]{2,1,0:T(8,128)(2,1)S(1)}, bf16[1,64,128]{2,1,0:T(8,128)(2,1)}, u32[]{:S(2)}) copy-start(bf16[1,64,128]{2,1,0:T(8,128)(2,1)} %param.12) | copy-start | bytes 49156
  15.6 8.1 %copy-start.8 = (f32[3,128]{1,0:T(4,128)S(1)}, f32[3,128]{1,0:T(4,128)}, u32[]{:S(2)}) copy-start(f32[3,128]{1,0:T(4,128)} %param.20) | copy-start | bytes 4612
  15.6 15.0 %all-to-all-start = ((bf16[16,16,128]{2,1,0:T(8,128)(2,1)}), bf16[16,16,128]{2,1,0:T(8,128)(2,1)S(1)}, u32[]{:S(2)}, u32[]{:S(2)}) async-start(bf16[16,16,128]{2,1,0:T(8,128)(2,1)} %bitcast.45), calls=%async_computation | async-start | bytes 131072 | tf_op jit(solution)/shard_map/all_to_all | solution.py:92
  30.6 0.8 %copy-start.4 = (bf16[128,128]{1,0:T(8,128)(2,1)S(1)}, bf16[128,128]{1,0:T(8,128)(2,1)}, u32[]{:S(2)}) copy-start(bf16[128,128]{1,0:T(8,128)(2,1)} %param.18) | copy-start | bytes 98308
  31.3 0.8 %copy-start.5 = (bf16[128,128]{1,0:T(8,128)(2,1)S(1)}, bf16[128,128]{1,0:T(8,128)(2,1)}, u32[]{:S(2)}) copy-start(bf16[128,128]{1,0:T(8,128)(2,1)} %param.19) | copy-start | bytes 98308
  32.6 1.0 %copy-start.9 = (bf16[3,512,128]{2,1,0:T(8,128)(2,1)S(1)}, bf16[3,512,128]{2,1,0:T(8,128)(2,1)}, u32[]{:S(2)}) copy-start(bf16[3,512,128]{2,1,0:T(8,128)(2,1)} %param.23) | copy-start | bytes 1179652
  32.6 1.1 %copy-start.10 = (bf16[3,128,512]{2,1,0:T(8,128)(2,1)S(1)}, bf16[3,128,512]{2,1,0:T(8,128)(2,1)}, u32[]{:S(2)}) copy-start(bf16[3,128,512]{2,1,0:T(8,128)(2,1)} %param.22) | copy-start | bytes 1179652
  37.5 13.5 %all-to-all-start.1 = ((bf16[16,64,128]{2,1,0:T(8,128)(2,1)}), bf16[16,64,128]{2,1,0:T(8,128)(2,1)S(1)}, u32[]{:S(2)}, u32[]{:S(2)}) async-start(bf16[16,64,128]{2,1,0:T(8,128)(2,1)} %constant_dynamic-update-slice_fusion), calls=%async_computation.1 | async-start | bytes 524288 | tf_op jit(solution)/shard_map/all_to_all | solution.py:100
  41.0 0.7 %copy-start.2 = (s32[4,8]{1,0:T(4,128)S(1)}, s32[4,8]{1,0:T(4,128)}, u32[]{:S(2)}) copy-start(s32[4,8]{1,0:T(4,128)} %param.15) | copy-start | bytes 388
where the time goes:
time: 52.8 us; the launch traced here: 52 us
  starting transfers between devices  16.1 us (30%)
  waiting for transfers between devices  15.4 us (29%)
  local copies, waits for them, and re-layouts  10.3 us (20%)
  between operations  4.86 us (9%)
  matrix products  3.94 us (7%)
  other arithmetic  1.47 us (3%)
    all_to_all x1, waiting for transfers between devices, on_device(): lax.all_to_all(placed, 'frame', split_axis=0, concat_axis=0, tiled=True)  8.51 us
    all_to_all x1, starting transfers between devices, on_device(): lax.all_to_all(outgoing, 'frame', split_axis=0, concat_axis=0, tiled=True)  8.08 us
    all_to_all x1, waiting for transfers between devices, on_device(): lax.all_to_all(outgoing, 'frame', split_axis=0, concat_axis=0, tiled=True)  6.87 us
    unnamed x25, local copies, waits for them, and re-layouts  5.51 us
    all_to_all x1, starting transfers between devices, on_device(): lax.all_to_all(placed, 'frame', split_axis=0, concat_axis=0, tiled=True)  3.53 us
    ppermute x1, starting transfers between devices, padded_2(): lax.ppermute(tail, axis, [(i, (i + 1) % count) for i in range(ends)])  3.04 us
    dot_general x3, matrix products, refine_block(): jnp.dot(hidden, mlp_out[layer_id], preferred_element_type=jnp.float32)  1.83 us
    ppermute x1, starting transfers between devices, padded_2(): lax.ppermute(head, axis, [((i + 1) % count, i) for i in range(ends)])  1.41 us
  transfers between devices with their start and end apart: 4, of which 2 were waited for; matrix products, arithmetic and copies ran while one was open for 8% of the time, Pallas kernels for 0%

commit v1 on v0

v1 whole, which is shorter than its diff:
```python
import functools

import jax
import jax.numpy as jnp
from jax import lax
from jax.experimental import pallas as pl
from jax.experimental.pallas import tpu as pltpu
from jax.sharding import PartitionSpec as P

AXIS = "frame"
UNROLL_UP_TO = 16


def each(count, body, carry=None):
    if count <= UNROLL_UP_TO:
        for index in range(count):
            carry = body(index, carry)
        return carry
    return lax.fori_loop(0, count, body, carry)


def kernel(
    chunks,
    lowres_hbm, noisy_hbm, starts_hbm, blend_hbm, assign_hbm, base_w_hbm, cond_w_hbm, noise_w_hbm,
    gains_hbm, tconv_hbm, mlp_in_hbm, mlp_out_hbm,
    out_ref,
    lowres, noisy, starts, blend, assign, base_w, cond_w, noise_w, gains, tconv, mlp_in, mlp_out,
    tile_out, tile_in, state_ref, lifted, refined, frames_out, frames_in, weights,
    load_sem, tile_send_sem, tile_recv_sem, frame_send_sem, frame_recv_sem,
):
    slots = assign.shape[0]
    windows, window_len = blend.shape
    tiles = slots // windows
    tile_pos, channels = noisy.shape[1], noisy.shape[2]
    low_pos = lowres.shape[1]
    ratio = tile_pos // low_pos
    layers = gains.shape[0]
    part = tile_pos // chunks
    me = lax.axis_index(AXIS)

    loads = {}
    for spot, (name, source, target) in enumerate((
        ("assign", assign_hbm, assign),
        ("lowres", lowres_hbm, lowres),
        ("starts", starts_hbm, starts),
        ("blend", blend_hbm, blend),
        ("noisy", noisy_hbm.at[0], noisy),
        ("noise_w", noise_w_hbm, noise_w),
        ("base_w", base_w_hbm, base_w),
        ("cond_w", cond_w_hbm, cond_w),
        ("gains", gains_hbm, gains),
        ("tconv", tconv_hbm, tconv),
        ("mlp_in", mlp_in_hbm, mlp_in),
        ("mlp_out", mlp_out_hbm, mlp_out),
    )):
        loads[name] = pltpu.make_async_copy(source, target, load_sem.at[spot])
        loads[name].start()

    def partner(step):
        half = slots // 2
        offset = half + (step + 1) // 2 * (1 - 2 * (step % 2))
        return lax.rem(me + offset + slots, slots)

    barrier = pltpu.get_barrier_semaphore()

    def greet(step, carry):
        pl.semaphore_signal(
            barrier, inc=1, device_id={AXIS: partner(step)}, device_id_type=pl.DeviceIdType.MESH
        )
        return carry

    each(slots - 1, greet)

    zero_tile = jnp.zeros((low_pos, channels), tile_in.dtype)
    tile_in[0] = zero_tile
    tile_in[slots + 1] = zero_tile
    loads["assign"].wait()
    loads["lowres"].wait()

    def tile_for(slot):
        return lowres[lax.rem(assign[slot], tiles)]

    def pick(slot, carry):
        tile_out[slot] = tile_for(slot)
        return carry

    each(slots, pick)
    tile_in[me + 1] = tile_for(me)

    pl.semaphore_wait(barrier, slots - 1)

    def send_tile(step, carry):
        there = partner(step)
        pltpu.make_async_remote_copy(
            src_ref=tile_out.at[there],
            dst_ref=tile_in.at[me + 1],
            send_sem=tile_send_sem,
            recv_sem=tile_recv_sem,
            device_id={AXIS: there},
            device_id_type=pl.DeviceIdType.MESH,
        ).start()
        return carry

    each(slots - 1, send_tile)

    loads["noisy"].wait()
    loads["noise_w"].wait()
    rows = window_len * tile_pos
    state_ref[...] = jnp.dot(
        noisy[...].reshape(rows, channels), noise_w[...], preferred_element_type=jnp.float32
    ).reshape(window_len, tile_pos, channels)

    loads["starts"].wait()
    loads["blend"].wait()

    def weigh(slot, total):
        item = assign[slot]
        window = lax.div(item, tiles)
        tile = lax.rem(item, tiles)
        offset = me - starts[window]
        inside = jnp.logical_and(offset >= 0, offset < window_len)
        value = blend[window, jnp.clip(offset, 0, window_len - 1)]
        value = jnp.where(inside, value, 0)
        for t in range(tiles):
            weights[slot * tiles + t] = jnp.where(tile == t, value, 0).astype(jnp.float32)
        return total + jnp.where(tile == 0, value, 0)

    denom = each(slots, weigh, jnp.int32(0)).astype(jnp.float32)
    start = starts[lax.div(assign[me], tiles)]

    loads["gains"].wait()
    loads["tconv"].wait()
    loads["base_w"].wait()
    loads["cond_w"].wait()
    pltpu.make_async_copy(
        tile_in.at[pl.ds(0, slots - 1)],
        tile_in.at[pl.ds(0, slots - 1)],
        tile_recv_sem,
    ).wait()

    low_rows = window_len * low_pos
    near = [tile_in[start + k] for k in range(window_len + 2)]
    seen = [jnp.concatenate(near[k : k + window_len], 0) for k in range(3)]
    total = jnp.dot(seen[0], base_w[0], preferred_element_type=jnp.float32)
    total = total + jnp.dot(seen[1], base_w[1], preferred_element_type=jnp.float32)
    total = total + jnp.dot(seen[2], base_w[2], preferred_element_type=jnp.float32)
    half = total * 0.5
    base = (seen[1].astype(jnp.float32) + (half + half * jnp.tanh(half))).astype(jnp.bfloat16)
    projected = jnp.dot(base, cond_w[...], preferred_element_type=jnp.float32)
    for r in range(ratio):
        lifted[pl.ds(r, low_rows, stride=ratio), :] = projected

    loads["mlp_in"].wait()
    loads["mlp_out"].wait()
    for c in range(chunks):
        span = pl.ds(c * part, part)
        state = state_ref[:, span, :] + lifted[...].reshape(window_len, tile_pos, channels)[
            :, c * part : (c + 1) * part
        ]
        zeros_frame = jnp.zeros((1, part, channels), jnp.float32)
        for layer in range(layers):
            inverse = lax.rsqrt(jnp.mean(state * state, axis=-1, keepdims=True) + 1e-06)
            plain = state * inverse
            gain = gains[pl.ds(layer, 1), :] * 0.5
            taps = tconv[layer]
            before = (taps[0:1] * gain).reshape(1, 1, channels)
            here = (gain + taps[1:2] * gain).reshape(1, 1, channels)
            behind = (taps[2:3] * gain).reshape(1, 1, channels)
            mixed = (
                here * plain
                + before * jnp.concatenate([zeros_frame, plain[:-1]], 0)
                + behind * jnp.concatenate([plain[1:], zeros_frame], 0)
            )
            mixed = mixed.reshape(window_len * part, channels).astype(jnp.bfloat16)
            half = jnp.dot(mixed, mlp_in[layer], preferred_element_type=jnp.float32)
            hidden = (half + half * jnp.tanh(half)).astype(jnp.bfloat16)
            state = state + jnp.dot(
                hidden, mlp_out[layer], preferred_element_type=jnp.float32
            ).reshape(window_len, part, channels)
        refined[c] = state.astype(jnp.bfloat16)

        def place(frame, carry, c=c):
            frames_out[c, frame] = refined[c, jnp.clip(frame - start, 0, window_len - 1)]
            return carry

        each(slots, place)
        frames_in[c, me] = refined[c, jnp.clip(me - start, 0, window_len - 1)]

        def send_frame(step, carry, c=c):
            there = partner(step)
            pltpu.make_async_remote_copy(
                src_ref=frames_out.at[c, there],
                dst_ref=frames_in.at[c, me],
                send_sem=frame_send_sem.at[c],
                recv_sem=frame_recv_sem.at[c],
                device_id={AXIS: there},
                device_id_type=pl.DeviceIdType.MESH,
            ).start()
            return carry

        each(slots - 1, send_frame)

    scale = jnp.full((1, channels), 1.0, jnp.float32) / jnp.full((1, channels), denom, jnp.float32)
    for c in range(chunks):
        arrived = frames_in.at[c, pl.ds(0, slots - 1)]
        pltpu.make_async_copy(arrived, arrived, frame_recv_sem.at[c]).wait()

        def add(slot, sums, c=c):
            value = frames_in[c, slot].astype(jnp.float32)
            return tuple(
                sums[t] + weights[slot * tiles + t] * value for t in range(tiles)
            )

        sums = each(slots, add, tuple(jnp.zeros((part, channels), jnp.float32) for _ in range(tiles)))
        for t in range(tiles):
            out_ref[0, pl.ds(t * tile_pos + c * part, part), :] = (sums[t] * scale).astype(
                out_ref.dtype
            )

    sent = tile_out.at[pl.ds(0, slots - 1)]
    pltpu.make_async_copy(sent, sent, tile_send_sem).wait()
    for c in range(chunks):
        sent = frames_out.at[c, pl.ds(0, slots - 1)]
        pltpu.make_async_copy(sent, sent, frame_send_sem.at[c]).wait()


def on_device(chunks, *args):
    (lowres, noisy, starts, blend, assign, base_w, cond_w, noise_w, gains, tconv, mlp_in,
     mlp_out) = args
    slots = assign.shape[0]
    windows = starts.shape[0]
    tiles = slots // windows
    _, window_len, tile_pos, channels = noisy.shape
    low_pos = lowres.shape[1] // tiles
    part = tile_pos // chunks
    half = jnp.bfloat16
    full = jnp.float32
    whole = jnp.int32
    return pl.pallas_call(
        functools.partial(kernel, chunks),
        out_shape=jax.ShapeDtypeStruct((1, tiles * tile_pos, channels), half),
        in_specs=[pl.BlockSpec(memory_space=pltpu.HBM)] * len(args),
        out_specs=pl.BlockSpec(memory_space=pltpu.VMEM),
        scratch_shapes=[
            pltpu.VMEM((tiles, low_pos, channels), half),
            pltpu.VMEM(noisy.shape[1:], half),
            pltpu.SMEM(starts.shape, whole),
            pltpu.SMEM(blend.shape, whole),
            pltpu.SMEM(assign.shape, whole),
            pltpu.VMEM(base_w.shape, half),
            pltpu.VMEM(cond_w.shape, half),
            pltpu.VMEM(noise_w.shape, half),
            pltpu.VMEM(gains.shape, full),
            pltpu.VMEM(tconv.shape, full),
            pltpu.VMEM(mlp_in.shape, half),
            pltpu.VMEM(mlp_out.shape, half),
            pltpu.VMEM((slots, low_pos, channels), half),
            pltpu.VMEM((slots + 2, low_pos, channels), half),
            pltpu.VMEM((window_len, tile_pos, channels), full),
            pltpu.VMEM((window_len * tile_pos, channels), full),
            pltpu.VMEM((chunks, window_len, part, channels), half),
            pltpu.VMEM((chunks, slots, part, channels), half),
            pltpu.VMEM((chunks, slots, part, channels), half),
            pltpu.SMEM((slots * tiles,), full),
            pltpu.SemaphoreType.DMA((len(args),)),
            pltpu.SemaphoreType.DMA,
            pltpu.SemaphoreType.DMA,
            pltpu.SemaphoreType.DMA((chunks,)),
            pltpu.SemaphoreType.DMA((chunks,)),
        ],
        compiler_params=pltpu.CompilerParams(
            collective_id=0, has_side_effects=True, vmem_limit_bytes=60 * 1024 * 1024
        ),
    )(lowres.reshape(tiles, low_pos, channels), *args[1:])


def solution(mesh):
    in_specs = (
        P(("groups", AXIS), None, None),
        P(("groups", AXIS), None, None, None),
        P("groups"),
        P("groups", None),
        P("groups"),
        P(),
        P(),
        P(),
        P(),
        P(),
        P(),
        P(),
    )
    out_specs = P(("groups", AXIS), None, None)
    return jax.shard_map(
        functools.partial(on_device, 2),
        mesh=mesh, in_specs=in_specs, out_specs=out_specs, check_vma=False
    )
```

time: 52.8 us -> 22.1 us (0.42); the launches traced: 52 us -> 21.9 us
  Pallas kernels: 0 us -> 20.5 us
  starting transfers between devices: 16.1 us -> 0 us
  waiting for transfers between devices: 15.4 us -> 0 us
  local copies, waits for them, and re-layouts: 10.3 us -> 1.47 us
  between operations: 4.86 us -> 0.01 us
  matrix products: 3.94 us -> 0 us
  other arithmetic: 1.47 us -> 0 us
    pallas_call x0 -> x1, Pallas kernels: none -> 20.5 us  [on_device(): pl.pallas_call(functools.partial(kernel, chunks), out_shape=jax.ShapeDtyp...]
    all_to_all x2 -> x0, waiting for transfers between devices: 15.4 us -> none  [the longest x1 8.51 us: on_device(): lax.all_to_all(placed, 'frame', split_axis=0, concat_axis=0, tiled=True)]
    all_to_all x2 -> x0, starting transfers between devices: 11.6 us -> none  [the longest x1 8.08 us: on_device(): lax.all_to_all(outgoing, 'frame', split_axis=0, concat_axis=0, tiled=True)]
    ppermute x2 -> x0, starting transfers between devices: 4.45 us -> none  [the longest x1 3.04 us: padded_2(): lax.ppermute(tail, axis, [(i, (i + 1) % count) for i in range(ends)])]
    unnamed x25 -> x1, local copies, waits for them, and re-layouts: 5.51 us -> 1.47 us
    dot_general x10 -> x0, matrix products: 3.94 us -> none  [the longest x3 1.83 us: refine_block(): jnp.dot(hidden, mlp_out[layer_id], preferred_element_type=jnp.float32)]
    gather x2 -> x0, local copies, waits for them, and re-layouts: 1.34 us -> none  [the longest x1 0.68 us: on_device(): blend[source_window, clipped]]
    dynamic_slice x3 -> x0, local copies, waits for them, and re-layouts: 1.17 us -> none  [the longest x1 0.58 us: on_device(): item_id = assign[own_index]]
  transfers between devices with their start and end apart: 4 -> 0, of which waited for: 2 -> 0; matrix products, arithmetic and copies ran while one was open for 8% -> 0% of each run, Pallas kernels for 0% -> 0%
where the time goes in v1:
time: 22.1 us; the launch traced here: 21.9 us
  Pallas kernels  20.5 us (93%)
  local copies, waits for them, and re-layouts  1.47 us (7%)
    pallas_call x1, Pallas kernels, on_device(): pl.pallas_call(functools.partial(kernel, chunks), out_shape=jax.ShapeDtyp...  20.5 us
    unnamed x1, local copies, waits for them, and re-layouts  1.47 us

profile of v1, /device:TPU:0, one launch (start us, length us, event | category | flops | bytes accessed | tf_op | source)
XLA Modules:
  0.0 21.9 jit_solution(6235903096609386874)
XLA Ops:
  0.0 20.5 %shard_map.118 = bf16[1,256,128]{2,1,0:T(8,128)(2,1)} custom-call(bf16[4,16,128]{2,1,0:T(8,128)(2,1)} %bitcast.1, bf16[1,8,64,128]{3,2,1,0:T(8,128)(2,1)} %noisy_hbm.1, s32[4]{0:T(128)} %starts_hbm.1, s32[4,8]{1,0:T(4,128)} %blend_hbm.1, s32[16]{0:T(128)} %assign_hbm.1, bf16[3,128,128]{2,1,0:T(8,128)(2,1)} %base_w_hbm.1, bf16[128,128]{1,0:T(8,128)(2,1)} %cond_w_hbm.1, ...), custom_call_target="tpu_custom_call" | custom-call | tf_op jit(solution)/shard_map/pallas_call | solution.py:239
  20.5 1.5 %copy.14 = bf16[1,256,128]{2,1,0:T(8,128)(2,1)} copy(bf16[1,256,128]{2,1,0:T(8,128)(2,1)} %shard_map.118) | data formatting | bytes 131072

commit v2 on v1

--- a/solution.py
+++ b/solution.py
@@ -238,7 +238,7 @@
     whole = jnp.int32
     return pl.pallas_call(
         functools.partial(kernel, chunks),
-        out_shape=jax.ShapeDtypeStruct((1, tiles * tile_pos, channels), half),
+        out_shape=jax.ShapeDtypeStruct((1, tiles * tile_pos, channels), full),
         in_specs=[pl.BlockSpec(memory_space=pltpu.HBM)] * len(args),
         out_specs=pl.BlockSpec(memory_space=pltpu.VMEM),
         scratch_shapes=[
@@ -271,7 +271,7 @@
         compiler_params=pltpu.CompilerParams(
             collective_id=0, has_side_effects=True, vmem_limit_bytes=60 * 1024 * 1024
         ),
-    )(lowres.reshape(tiles, low_pos, channels), *args[1:])
+    )(lowres.reshape(tiles, low_pos, channels), *args[1:]).astype(half)
 
 
 def solution(mesh):
@@ -291,6 +291,6 @@
     )
     out_specs = P(("groups", AXIS), None, None)
     return jax.shard_map(
-        functools.partial(on_device, 2),
+        functools.partial(on_device, 4),
         mesh=mesh, in_specs=in_specs, out_specs=out_specs, check_vma=False
     )

time: 22.1 us -> 22.6 us (1.023)
  other arithmetic: 0 us -> 1.54 us
  local copies, waits for them, and re-layouts: 1.47 us -> 0 us
  Pallas kernels: 20.5 us -> 20.9 us
    convert_element_type x0 -> x1, other arithmetic: none -> 1.54 us  [on_device(): return pl.pallas_call(functools.partial(kernel, chunks), out_shape=jax.Sh...]
    unnamed x1 -> x0, local copies, waits for them, and re-layouts: 1.47 us -> none
    pallas_call x1, Pallas kernels: 20.5 us -> 20.9 us  [on_device(): pl.pallas_call(functools.partial(kernel, chunks), out_shape=jax.ShapeDtyp...]
where the time goes in v2:
time: 22.6 us; the launch traced here: 22.5 us
  Pallas kernels  20.9 us (92%)
  other arithmetic  1.54 us (7%)
    pallas_call x1, Pallas kernels, on_device(): pl.pallas_call(functools.partial(kernel, chunks), out_shape=jax.ShapeDtyp...  20.9 us
    convert_element_type x1, other arithmetic, on_device(): return pl.pallas_call(functools.partial(kernel, chunks), out_shape=jax.Sh...  1.54 us

profile of v2, /device:TPU:0, one launch (start us, length us, event | category | flops | bytes accessed | tf_op | source)
XLA Modules:
  0.0 22.5 jit_solution(18188311127031703739)
XLA Ops:
  0.0 20.9 %shard_map.118 = f32[1,256,128]{2,1,0:T(8,128)} custom-call(bf16[4,16,128]{2,1,0:T(8,128)(2,1)} %bitcast.1, bf16[1,8,64,128]{3,2,1,0:T(8,128)(2,1)} %noisy_hbm.1, s32[4]{0:T(128)} %starts_hbm.1, s32[4,8]{1,0:T(4,128)} %blend_hbm.1, s32[16]{0:T(128)} %assign_hbm.1, bf16[3,128,128]{2,1,0:T(8,128)(2,1)} %base_w_hbm.1, bf16[128,128]{1,0:T(8,128)(2,1)} %cond_w_hbm.1, ...), custom_call_target="tpu_custom_call" | custom-call | tf_op jit(solution)/shard_map/pallas_call | solution.py:239
  20.9 1.5 %convert_element_type.3 = bf16[1,256,128]{2,1,0:T(8,128)(2,1)} convert(f32[1,256,128]{2,1,0:T(8,128)} %shard_map.118) | non-fusion elementwise | flops 32768 | bytes 196608 | tf_op jit(solution)/shard_map/convert_element_type | solution.py:274

commit v3 on v1

--- a/solution.py
+++ b/solution.py
@@ -9,6 +9,7 @@
 
 AXIS = "frame"
 UNROLL_UP_TO = 16
+SUBLANES = 8
 
 
 def each(count, body, carry=None):
@@ -19,7 +20,7 @@
     return lax.fori_loop(0, count, body, carry)
 
 
-def kernel(
+def slot_kernel(
     chunks,
     lowres_hbm, noisy_hbm, starts_hbm, blend_hbm, assign_hbm, base_w_hbm, cond_w_hbm, noise_w_hbm,
     gains_hbm, tconv_hbm, mlp_in_hbm, mlp_out_hbm,
@@ -224,7 +225,7 @@
         pltpu.make_async_copy(sent, sent, frame_send_sem.at[c]).wait()
 
 
-def on_device(chunks, *args):
+def slot_on_device(chunks, *args):
     (lowres, noisy, starts, blend, assign, base_w, cond_w, noise_w, gains, tconv, mlp_in,
      mlp_out) = args
     slots = assign.shape[0]
@@ -237,7 +238,7 @@
     full = jnp.float32
     whole = jnp.int32
     return pl.pallas_call(
-        functools.partial(kernel, chunks),
+        functools.partial(slot_kernel, chunks),
         out_shape=jax.ShapeDtypeStruct((1, tiles * tile_pos, channels), half),
         in_specs=[pl.BlockSpec(memory_space=pltpu.HBM)] * len(args),
         out_specs=pl.BlockSpec(memory_space=pltpu.VMEM),
@@ -274,6 +275,249 @@
     )(lowres.reshape(tiles, low_pos, channels), *args[1:])
 
 
+def split_kernel(
+    lowres_hbm, noisy_hbm, starts_hbm, blend_hbm, assign_hbm, base_w_hbm, cond_w_hbm, noise_w_hbm,
+    gains_hbm, tconv_hbm, mlp_in_hbm, mlp_out_hbm,
+    out_ref,
+    lowres, noisy, starts, blend, assign, base_w, cond_w, noise_w, gains, tconv, mlp_in, mlp_out,
+    low_out, low_in, noisy_wide, noisy_out, noisy_in, projected, shifted, cond_ref,
+    video_out, video_in, video_wide,
+    load_sem, low_send, low_recv, noisy_send, noisy_recv, video_send, video_recv,
+):
+    slots = assign.shape[0]
+    windows, window_len = blend.shape
+    tiles, low_pos, channels = lowres.shape
+    tile_pos = noisy.shape[1]
+    ratio = tile_pos // low_pos
+    layers = gains.shape[0]
+    pad = low_out.shape[0] // slots
+    me = lax.axis_index(AXIS)
+
+    loads = {}
+    for spot, (name, source, target) in enumerate((
+        ("lowres", lowres_hbm, lowres),
+        ("noisy", noisy_hbm.at[0], noisy),
+        ("assign", assign_hbm, assign),
+        ("starts", starts_hbm, starts),
+        ("blend", blend_hbm, blend),
+        ("base_w", base_w_hbm, base_w),
+        ("cond_w", cond_w_hbm, cond_w),
+        ("noise_w", noise_w_hbm, noise_w),
+        ("gains", gains_hbm, gains),
+        ("tconv", tconv_hbm, tconv),
+        ("mlp_in", mlp_in_hbm, mlp_in),
+        ("mlp_out", mlp_out_hbm, mlp_out),
+    )):
+        loads[name] = pltpu.make_async_copy(source, target, load_sem.at[spot])
+        loads[name].start()
+
+    partners = []
+    for step in range(slots - 1):
+        offset = slots // 2 + (step + 1) // 2 * (1 - 2 * (step % 2))
+        partners.append(lax.rem(me + offset, slots))
+
+    barrier = pltpu.get_barrier_semaphore()
+    for there in partners:
+        pl.semaphore_signal(
+            barrier, inc=1, device_id={AXIS: there}, device_id_type=pl.DeviceIdType.MESH
+        )
+
+    def send(source, target, there, send_sem, recv_sem):
+        pltpu.make_async_remote_copy(
+            src_ref=source, dst_ref=target, send_sem=send_sem, recv_sem=recv_sem,
+            device_id={AXIS: there}, device_id_type=pl.DeviceIdType.MESH,
+        ).start()
+
+    def await_bytes(ref, sem):
+        pltpu.make_async_copy(ref, ref, sem).wait()
+
+    def block(index, rows):
+        return pl.ds(pl.multiple_of(index * rows, rows), rows)
+
+    low_out[...] = jnp.zeros_like(low_out)
+    zero_pad = jnp.zeros((pad, channels), jnp.float32)
+    low_in[pl.ds(0, pad), :] = zero_pad
+    low_in[pl.ds((slots + 1) * pad, pad), :] = zero_pad
+    loads["lowres"].wait()
+    for t in range(tiles):
+        low_out[pl.ds(t, low_pos, stride=pad), :] = lowres[t].astype(jnp.float32)
+    low_in[block(me + 1, pad), :] = low_out[block(me, pad), :]
+
+    loads["noisy"].wait()
+    noisy_wide[...] = noisy[...].reshape(window_len * tile_pos, channels).astype(jnp.float32)
+    for j in range(slots):
+        picked = [
+            noisy_wide[pl.ds(j * ratio + r, window_len, stride=tile_pos), :] for r in range(ratio)
+        ]
+        noisy_out[j] = jnp.concatenate(picked, 0).astype(jnp.bfloat16)
+    noisy_in[me] = noisy_out[me]
+
+    pl.semaphore_wait(barrier, slots - 1)
+    for there in partners:
+        send(low_out.at[block(there, pad)], low_in.at[block(me + 1, pad)], there, low_send, low_recv)
+    for there in partners:
+        send(noisy_out.at[there], noisy_in.at[me], there, noisy_send, noisy_recv)
+
+    for name in ("assign", "starts", "blend"):
+        loads[name].wait()
+    rows = slots * ratio * window_len
+    lane = lax.broadcasted_iota(jnp.int32, (1, rows), 1)
+    lane_slot = lane // (ratio * window_len)
+    lane_pos = (lane // window_len) % ratio
+    lane_step = lane % window_len
+    first = jnp.zeros((1, rows), jnp.int32)
+    lane_tile = jnp.zeros((1, rows), jnp.int32)
+    lane_window = jnp.zeros((1, rows), jnp.int32)
+    for d in range(slots):
+        item = assign[d]
+        here = lane_slot == d
+        window = lax.div(item, tiles)
+        lane_window = jnp.where(here, window, lane_window)
+        lane_tile = jnp.where(here, lax.rem(item, tiles), lane_tile)
+        first = jnp.where(here, starts[window], first)
+    factor = jnp.zeros((1, rows), jnp.int32)
+    for w in range(windows):
+        for k in range(window_len):
+            factor = jnp.where(
+                jnp.logical_and(lane_window == w, lane_step == k), blend[w, k], factor
+            )
+    target = ((first + lane_step) * tiles + lane_tile) * ratio + lane_pos
+    video_rows = slots * tiles * ratio
+    row = lax.broadcasted_iota(jnp.int32, (video_rows, rows), 0)
+    matrix = jnp.where(row == target, factor.astype(jnp.float32), 0.0)
+    denom = jnp.sum(matrix, axis=1, keepdims=True)
+    matrix = matrix.astype(jnp.bfloat16)
+
+    for name in ("base_w", "cond_w", "noise_w", "gains", "tconv"):
+        loads[name].wait()
+    await_bytes(low_in.at[pl.ds(0, (slots - 1) * pad)], low_recv)
+    total = None
+    for k in range(3):
+        seen = jnp.concatenate(
+            [low_in[pl.ds(k * pad + t, slots, stride=pad), :] for t in range(tiles)], 0
+        )
+        if k == 1:
+            centre = seen
+        term = jnp.dot(seen.astype(jnp.bfloat16), base_w[k], preferred_element_type=jnp.float32)
+        total = term if total is None else total + term
+    half = total * 0.5
+    base = (centre + (half + half * jnp.tanh(half))).astype(jnp.bfloat16)
+    projected[...] = jnp.dot(base, cond_w[...], preferred_element_type=jnp.float32)
+    for t in range(tiles):
+        for f in range(slots - window_len + 1):
+            shifted[t, f] = projected[pl.ds(t * slots + f, window_len), :]
+    for d in range(slots):
+        item = assign[d]
+        cond_ref[d, 0] = shifted[lax.rem(item, tiles), starts[lax.div(item, tiles)]]
+
+    loads["mlp_in"].wait()
+    loads["mlp_out"].wait()
+    await_bytes(noisy_in.at[pl.ds(0, slots - 1)], noisy_recv)
+    state = jnp.dot(
+        noisy_in[...].reshape(rows, channels), noise_w[...], preferred_element_type=jnp.float32
+    ).reshape(slots, ratio, window_len, channels)
+    state = (state + cond_ref[...]).reshape(slots * ratio, window_len, channels)
+    step_row = lax.broadcasted_iota(jnp.int32, (window_len, channels), 0)
+    for layer in range(layers):
+        inverse = lax.rsqrt(jnp.mean(state * state, axis=-1, keepdims=True) + 1e-06)
+        plain = state * inverse
+        gain = gains[pl.ds(layer, 1), :] * 0.5
+        taps = tconv[layer]
+        before = jnp.where(step_row == 0, 0.0, taps[0:1] * gain)
+        here = gain + taps[1:2] * gain
+        behind = jnp.where(step_row == window_len - 1, 0.0, taps[2:3] * gain)
+        mixed = (
+            here[None] * plain
+            + before[None] * pltpu.roll(plain, 1, 1)
+            + behind[None] * pltpu.roll(plain, window_len - 1, 1)
+        )
+        mixed = mixed.reshape(rows, channels).astype(jnp.bfloat16)
+        half = jnp.dot(mixed, mlp_in[layer], preferred_element_type=jnp.float32)
+        hidden = (half + half * jnp.tanh(half)).astype(jnp.bfloat16)
+        state = state + jnp.dot(
+            hidden, mlp_out[layer], preferred_element_type=jnp.float32
+        ).reshape(slots * ratio, window_len, channels)
+    refined = state.reshape(rows, channels).astype(jnp.bfloat16)
+    video = jnp.dot(matrix, refined, preferred_element_type=jnp.float32) / denom
+    video_out[...] = video.astype(jnp.bfloat16).reshape(slots, tiles * ratio, channels)
+    video_in[me] = video_out[me]
+    for there in partners:
+        send(video_out.at[there], video_in.at[me], there, video_send, video_recv)
+
+    await_bytes(low_out.at[pl.ds(0, (slots - 1) * pad)], low_send)
+    await_bytes(noisy_out.at[pl.ds(0, slots - 1)], noisy_send)
+    await_bytes(video_in.at[pl.ds(0, slots - 1)], video_recv)
+    video_wide[...] = video_in[...].reshape(video_rows, channels).astype(jnp.float32)
+    for t in range(tiles):
+        for r in range(ratio):
+            out_ref[0, pl.ds(t * tile_pos + r, low_pos, stride=ratio), :] = video_wide[
+                pl.ds(t * ratio + r, low_pos, stride=tiles * ratio), :
+            ]
+    await_bytes(video_out.at[pl.ds(0, slots - 1)], video_send)
+
+
+def split_on_device(*args):
+    (lowres, noisy, starts, blend, assign, base_w, cond_w, noise_w, gains, tconv, mlp_in,
+     mlp_out) = args
+    slots = assign.shape[0]
+    tiles = slots // starts.shape[0]
+    _, window_len, tile_pos, channels = noisy.shape
+    low_pos = lowres.shape[1] // tiles
+    ratio = tile_pos // low_pos
+    rows = slots * ratio * window_len
+    half, full, whole = jnp.bfloat16, jnp.float32, jnp.int32
+    dma = pltpu.SemaphoreType.DMA
+    return pl.pallas_call(
+        split_kernel,
+        out_shape=jax.ShapeDtypeStruct((1, tiles * tile_pos, channels), full),
+        in_specs=[pl.BlockSpec(memory_space=pl.ANY)] * len(args),
+        out_specs=pl.BlockSpec(memory_space=pltpu.VMEM),
+        scratch_shapes=[
+            pltpu.VMEM((tiles, low_pos, channels), half),
+            pltpu.VMEM(noisy.shape[1:], half),
+            pltpu.SMEM(starts.shape, whole),
+            pltpu.SMEM(blend.shape, whole),
+            pltpu.SMEM(assign.shape, whole),
+            pltpu.VMEM(base_w.shape, half),
+            pltpu.VMEM(cond_w.shape, half),
+            pltpu.VMEM(noise_w.shape, half),
+            pltpu.VMEM(gains.shape, full),
+            pltpu.VMEM(tconv.shape, full),
+            pltpu.VMEM(mlp_in.shape, half),
+            pltpu.VMEM(mlp_out.shape, half),
+            pltpu.VMEM((slots * SUBLANES, channels), full),
+            pltpu.VMEM(((slots + 2) * SUBLANES, channels), full),
+            pltpu.VMEM((window_len * tile_pos, channels), full),
+            pltpu.VMEM((slots, ratio * window_len, channels), half),
+            pltpu.VMEM((slots, ratio * window_len, channels), half),
+            pltpu.VMEM((tiles * slots, channels), full),
+            pltpu.VMEM((tiles, slots - window_len + 1, window_len, channels), full),
+            pltpu.VMEM((slots, 1, window_len, channels), full),
+            pltpu.VMEM((slots, tiles * ratio, channels), half),
+            pltpu.VMEM((slots, tiles * ratio, channels), half),
+            pltpu.VMEM((slots * tiles * ratio, channels), full),
+            dma((len(args),)), dma, dma, dma, dma, dma, dma,
+        ],
+        compiler_params=pltpu.CompilerParams(
+            collective_id=0, has_side_effects=True, vmem_limit_bytes=60 * 1024 * 1024
+        ),
+    )(lowres.reshape(tiles, low_pos, channels), *args[1:]).astype(half)
+
+
+def on_device(*args):
+    lowres, noisy, starts, _, assign = args[:5]
+    slots = assign.shape[0]
+    tiles = slots // starts.shape[0]
+    low_pos = lowres.shape[1] // tiles
+    ratio = noisy.shape[2] // low_pos
+    if (
+        low_pos == slots and tiles <= SUBLANES and noisy.shape[1] == SUBLANES
+        and (tiles * ratio) % 16 == 0
+    ):
+        return split_on_device(*args)
+    return slot_on_device(2, *args)
+
+
 def solution(mesh):
     in_specs = (
         P(("groups", AXIS), None, None),
@@ -291,6 +535,6 @@
     )
     out_specs = P(("groups", AXIS), None, None)
     return jax.shard_map(
-        functools.partial(on_device, 2),
+        on_device,
         mesh=mesh, in_specs=in_specs, out_specs=out_specs, check_vma=False
     )

time: 22.1 us -> 21.2 us (0.959)
  other arithmetic: 0 us -> 1.54 us
  local copies, waits for them, and re-layouts: 1.47 us -> 0 us
  Pallas kernels: 20.5 us -> 19.4 us
    convert_element_type x0 -> x1, other arithmetic: none -> 1.54 us  [split_on_device(): return pl.pallas_call(split_kernel, out_shape=jax.ShapeDtypeStruct((1, ti...]
    unnamed x1 -> x0, local copies, waits for them, and re-layouts: 1.47 us -> none
    pallas_call x1, Pallas kernels: 20.5 us -> 19.4 us  [split_on_device(): pl.pallas_call(split_kernel, out_shape=jax.ShapeDtypeStruct((1, tiles * t...]
where the time goes in v3:
time: 21.2 us; the launch traced here: 21 us
  Pallas kernels  19.4 us (92%)
  other arithmetic  1.54 us (7%)
    pallas_call x1, Pallas kernels, split_on_device(): pl.pallas_call(split_kernel, out_shape=jax.ShapeDtypeStruct((1, tiles * t...  19.4 us
    convert_element_type x1, other arithmetic, split_on_device(): return pl.pallas_call(split_kernel, out_shape=jax.ShapeDtypeStruct((1, ti...  1.54 us

profile of v3, /device:TPU:0, one launch (start us, length us, event | category | flops | bytes accessed | tf_op | source)
XLA Modules:
  0.0 21.0 jit_solution(5583605315016014687)
XLA Ops:
  0.0 19.4 %shard_map.118 = f32[1,256,128]{2,1,0:T(8,128)} custom-call(bf16[4,16,128]{2,1,0:T(8,128)(2,1)} %bitcast.1, bf16[1,8,64,128]{3,2,1,0:T(8,128)(2,1)} %noisy_hbm.1, s32[4]{0:T(128)} %starts_hbm.1, s32[4,8]{1,0:T(4,128)} %blend_hbm.1, s32[16]{0:T(128)} %assign_hbm.1, bf16[3,128,128]{2,1,0:T(8,128)(2,1)} %base_w_hbm.1, bf16[128,128]{1,0:T(8,128)(2,1)} %cond_w_hbm.1, ...), custom_call_target="tpu_custom_call" | custom-call | tf_op jit(solution)/shard_map/pallas_call | solution.py:470
  19.4 1.5 %convert_element_type.3 = bf16[1,256,128]{2,1,0:T(8,128)(2,1)} convert(f32[1,256,128]{2,1,0:T(8,128)} %shard_map.118) | non-fusion elementwise | flops 32768 | bytes 196608 | tf_op jit(solution)/shard_map/convert_element_type | solution.py:504

commit v4 on v3

--- a/solution.py
+++ b/solution.py
@@ -281,8 +281,8 @@
     out_ref,
     lowres, noisy, starts, blend, assign, base_w, cond_w, noise_w, gains, tconv, mlp_in, mlp_out,
     low_out, low_in, noisy_wide, noisy_out, noisy_in, projected, shifted, cond_ref,
-    video_out, video_in, video_wide,
-    load_sem, low_send, low_recv, noisy_send, noisy_recv, video_send, video_recv,
+    video_out,
+    load_sem, low_send, low_recv, noisy_send, noisy_recv, video_send, video_recv, own_sem,
 ):
     slots = assign.shape[0]
     windows, window_len = blend.shape
@@ -290,7 +290,6 @@
     tile_pos = noisy.shape[1]
     ratio = tile_pos // low_pos
     layers = gains.shape[0]
-    pad = low_out.shape[0] // slots
     me = lax.axis_index(AXIS)
 
     loads = {}
@@ -331,17 +330,13 @@
     def await_bytes(ref, sem):
         pltpu.make_async_copy(ref, ref, sem).wait()
 
-    def block(index, rows):
-        return pl.ds(pl.multiple_of(index * rows, rows), rows)
-
-    low_out[...] = jnp.zeros_like(low_out)
-    zero_pad = jnp.zeros((pad, channels), jnp.float32)
-    low_in[pl.ds(0, pad), :] = zero_pad
-    low_in[pl.ds((slots + 1) * pad, pad), :] = zero_pad
+    zero_slab = jnp.zeros((tiles, channels), jnp.float32)
+    low_in[0] = zero_slab
+    low_in[slots + 1] = zero_slab
     loads["lowres"].wait()
     for t in range(tiles):
-        low_out[pl.ds(t, low_pos, stride=pad), :] = lowres[t].astype(jnp.float32)
-    low_in[block(me + 1, pad), :] = low_out[block(me, pad), :]
+        low_out[:, t, :] = lowres[t].astype(jnp.float32)
+    low_in[me + 1] = low_out[me]
 
     loads["noisy"].wait()
     noisy_wide[...] = noisy[...].reshape(window_len * tile_pos, channels).astype(jnp.float32)
@@ -354,7 +349,7 @@
 
     pl.semaphore_wait(barrier, slots - 1)
     for there in partners:
-        send(low_out.at[block(there, pad)], low_in.at[block(me + 1, pad)], there, low_send, low_recv)
+        send(low_out.at[there], low_in.at[me + 1], there, low_send, low_recv)
     for there in partners:
         send(noisy_out.at[there], noisy_in.at[me], there, noisy_send, noisy_recv)
 
@@ -390,11 +385,11 @@
 
     for name in ("base_w", "cond_w", "noise_w", "gains", "tconv"):
         loads[name].wait()
-    await_bytes(low_in.at[pl.ds(0, (slots - 1) * pad)], low_recv)
+    await_bytes(low_in.at[pl.ds(0, slots - 1)], low_recv)
     total = None
     for k in range(3):
         seen = jnp.concatenate(
-            [low_in[pl.ds(k * pad + t, slots, stride=pad), :] for t in range(tiles)], 0
+            [low_in[k : k + slots, t, :] for t in range(tiles)], 0
         )
         if k == 1:
             centre = seen
@@ -440,20 +435,29 @@
     refined = state.reshape(rows, channels).astype(jnp.bfloat16)
     video = jnp.dot(matrix, refined, preferred_element_type=jnp.float32) / denom
     video_out[...] = video.astype(jnp.bfloat16).reshape(slots, tiles * ratio, channels)
-    video_in[me] = video_out[me]
     for there in partners:
-        send(video_out.at[there], video_in.at[me], there, video_send, video_recv)
-
-    await_bytes(low_out.at[pl.ds(0, (slots - 1) * pad)], low_send)
+        send(video_out.at[there], out_ref.at[me], there, video_send, video_recv)
+    own = pltpu.make_async_copy(video_out.at[me], out_ref.at[me], own_sem)
+    own.start()
+
+    await_bytes(low_out.at[pl.ds(0, slots - 1)], low_send)
     await_bytes(noisy_out.at[pl.ds(0, slots - 1)], noisy_send)
-    await_bytes(video_in.at[pl.ds(0, slots - 1)], video_recv)
-    video_wide[...] = video_in[...].reshape(video_rows, channels).astype(jnp.float32)
+    await_bytes(out_ref.at[pl.ds(0, slots - 1)], video_recv)
+    own.wait()
+    await_bytes(video_out.at[pl.ds(0, slots - 1)], video_send)
+
+
+def order_kernel(tiles, video_ref, out_ref, wide, ordered):
+    sources, rows, channels = video_ref.shape
+    ratio = rows // tiles
+    tile_pos = sources * ratio
+    wide[...] = video_ref[...].reshape(sources * rows, channels).astype(jnp.float32)
     for t in range(tiles):
         for r in range(ratio):
-            out_ref[0, pl.ds(t * tile_pos + r, low_pos, stride=ratio), :] = video_wide[
-                pl.ds(t * ratio + r, low_pos, stride=tiles * ratio), :
+            ordered[pl.ds(t * tile_pos + r, sources, stride=ratio), :] = wide[
+                pl.ds(t * ratio + r, sources, stride=rows), :
             ]
-    await_bytes(video_out.at[pl.ds(0, slots - 1)], video_send)
+    out_ref[0] = ordered[...].astype(out_ref.dtype)
 
 
 def split_on_device(*args):
@@ -467,11 +471,11 @@
     rows = slots * ratio * window_len
     half, full, whole = jnp.bfloat16, jnp.float32, jnp.int32
     dma = pltpu.SemaphoreType.DMA
-    return pl.pallas_call(
+    video = pl.pallas_call(
         split_kernel,
-        out_shape=jax.ShapeDtypeStruct((1, tiles * tile_pos, channels), full),
+        out_shape=jax.ShapeDtypeStruct((slots, tiles * ratio, channels), half),
         in_specs=[pl.BlockSpec(memory_space=pl.ANY)] * len(args),
-        out_specs=pl.BlockSpec(memory_space=pltpu.VMEM),
+        out_specs=pl.BlockSpec(memory_space=pl.ANY),
         scratch_shapes=[
             pltpu.VMEM((tiles, low_pos, channels), half),
             pltpu.VMEM(noisy.shape[1:], half),
@@ -485,8 +489,8 @@
             pltpu.VMEM(tconv.shape, full),
             pltpu.VMEM(mlp_in.shape, half),
             pltpu.VMEM(mlp_out.shape, half),
-            pltpu.VMEM((slots * SUBLANES, channels), full),
-            pltpu.VMEM(((slots + 2) * SUBLANES, channels), full),
+            pltpu.VMEM((slots, tiles, channels), full),
+            pltpu.VMEM((slots + 2, tiles, channels), full),
             pltpu.VMEM((window_len * tile_pos, channels), full),
             pltpu.VMEM((slots, ratio * window_len, channels), half),
             pltpu.VMEM((slots, ratio * window_len, channels), half),
@@ -494,14 +498,23 @@
             pltpu.VMEM((tiles, slots - window_len + 1, window_len, channels), full),
             pltpu.VMEM((slots, 1, window_len, channels), full),
             pltpu.VMEM((slots, tiles * ratio, channels), half),
-            pltpu.VMEM((slots, tiles * ratio, channels), half),
-            pltpu.VMEM((slots * tiles * ratio, channels), full),
-            dma((len(args),)), dma, dma, dma, dma, dma, dma,
+            dma((len(args),)), dma, dma, dma, dma, dma, dma, dma,
         ],
         compiler_params=pltpu.CompilerParams(
             collective_id=0, has_side_effects=True, vmem_limit_bytes=60 * 1024 * 1024
         ),
-    )(lowres.reshape(tiles, low_pos, channels), *args[1:]).astype(half)
+    )(lowres.reshape(tiles, low_pos, channels), *args[1:])
+    return pl.pallas_call(
+        functools.partial(order_kernel, tiles),
+        out_shape=jax.ShapeDtypeStruct((1, tiles * tile_pos, channels), half),
+        in_specs=[pl.BlockSpec(memory_space=pltpu.VMEM)],
+        out_specs=pl.BlockSpec(memory_space=pltpu.VMEM),
+        scratch_shapes=[
+            pltpu.VMEM((tiles * tile_pos, channels), full),
+            pltpu.VMEM((tiles * tile_pos, channels), full),
+        ],
+        compiler_params=pltpu.CompilerParams(vmem_limit_bytes=60 * 1024 * 1024),
+    )(video)
 
 
 def on_device(*args):

time: 21.2 us -> 20.1 us (0.948)
  other arithmetic: 1.54 us -> 0 us
  Pallas kernels: 19.4 us -> 19.9 us
    convert_element_type x1 -> x0, other arithmetic: 1.54 us -> none  [split_on_device(): return pl.pallas_call(split_kernel, out_shape=jax.ShapeDtypeStruct((1, ti...]
    pallas_call x1 -> x2, Pallas kernels: 19.4 us -> 19.9 us  [the longest x1 18.3 us: split_on_device(): pl.pallas_call(split_kernel, out_shape=jax.ShapeDtypeStruct((slots, tiles...]
where the time goes in v4:
time: 20.1 us; the launch traced here: 19.9 us
  Pallas kernels  19.9 us (99%)
    pallas_call x1, Pallas kernels, split_on_device(): pl.pallas_call(split_kernel, out_shape=jax.ShapeDtypeStruct((slots, tiles...  18.3 us
    pallas_call x1, Pallas kernels, split_on_device(): pl.pallas_call(functools.partial(order_kernel, tiles), out_shape=jax.Shap...  1.53 us

profile of v4, /device:TPU:0, one launch (start us, length us, event | category | flops | bytes accessed | tf_op | source)
XLA Modules:
  0.0 19.9 jit_solution(5222113884915189059)
XLA Ops:
  0.0 18.3 %shard_map.118.video_ref = bf16[16,16,128]{2,1,0:T(8,128)(2,1)} custom-call(bf16[4,16,128]{2,1,0:T(8,128)(2,1)} %bitcast.1, bf16[1,8,64,128]{3,2,1,0:T(8,128)(2,1)} %noisy_hbm.1, s32[4]{0:T(128)} %starts_hbm.1, s32[4,8]{1,0:T(4,128)} %blend_hbm.1, s32[16]{0:T(128)} %assign_hbm.1, bf16[3,128,128]{2,1,0:T(8,128)(2,1)} %base_w_hbm.1, ...), custom_call_target="tpu_custom_call" | custom-call | tf_op jit(solution)/shard_map/pallas_call | solution.py:474
  18.3 1.5 %shard_map.119 = bf16[1,256,128]{2,1,0:T(8,128)(2,1)} custom-call(bf16[16,16,128]{2,1,0:T(8,128)(2,1)} %shard_map.118.video_ref), custom_call_target="tpu_custom_call" | custom-call | tf_op jit(solution)/shard_map/pallas_call | solution.py:507

commit v5 on v4

--- a/solution.py
+++ b/solution.py
@@ -281,7 +281,7 @@
     out_ref,
     lowres, noisy, starts, blend, assign, base_w, cond_w, noise_w, gains, tconv, mlp_in, mlp_out,
     low_out, low_in, noisy_wide, noisy_out, noisy_in, projected, shifted, cond_ref,
-    video_out,
+    video_out, matrices,
     load_sem, low_send, low_recv, noisy_send, noisy_recv, video_send, video_recv, own_sem,
 ):
     slots = assign.shape[0]
@@ -310,10 +310,15 @@
         loads[name] = pltpu.make_async_copy(source, target, load_sem.at[spot])
         loads[name].start()
 
-    partners = []
-    for step in range(slots - 1):
-        offset = slots // 2 + (step + 1) // 2 * (1 - 2 * (step % 2))
-        partners.append(lax.rem(me + offset, slots))
+    half_slots = slots // 2
+    side, place = me // half_slots, me % half_slots
+    away = [
+        (1 - side) * half_slots + lax.rem(place + step, half_slots) for step in range(half_slots)
+    ]
+    near = [
+        side * half_slots + lax.rem(place + step, half_slots) for step in range(1, half_slots)
+    ]
+    partners = away + near
 
     barrier = pltpu.get_barrier_semaphore()
     for there in partners:
@@ -345,13 +350,17 @@
             noisy_wide[pl.ds(j * ratio + r, window_len, stride=tile_pos), :] for r in range(ratio)
         ]
         noisy_out[j] = jnp.concatenate(picked, 0).astype(jnp.bfloat16)
-    noisy_in[me] = noisy_out[me]
+    noisy_in[side, place] = noisy_out[me]
 
     pl.semaphore_wait(barrier, slots - 1)
     for there in partners:
         send(low_out.at[there], low_in.at[me + 1], there, low_send, low_recv)
-    for there in partners:
-        send(noisy_out.at[there], noisy_in.at[me], there, noisy_send, noisy_recv)
+    for group, targets in enumerate((near, away)):
+        for there in targets:
+            send(
+                noisy_out.at[there], noisy_in.at[side, place], there,
+                noisy_send, noisy_recv.at[group],
+            )
 
     for name in ("assign", "starts", "blend"):
         loads[name].wait()
@@ -381,7 +390,10 @@
     row = lax.broadcasted_iota(jnp.int32, (video_rows, rows), 0)
     matrix = jnp.where(row == target, factor.astype(jnp.float32), 0.0)
     denom = jnp.sum(matrix, axis=1, keepdims=True)
-    matrix = matrix.astype(jnp.bfloat16)
+    scale = 1.0 / denom
+    half_rows = rows // 2
+    for h in range(2):
+        matrices[h] = matrix[:, h * half_rows : (h + 1) * half_rows].astype(jnp.bfloat16)
 
     for name in ("base_w", "cond_w", "noise_w", "gains", "tconv"):
         loads[name].wait()
@@ -403,37 +415,43 @@
             shifted[t, f] = projected[pl.ds(t * slots + f, window_len), :]
     for d in range(slots):
         item = assign[d]
-        cond_ref[d, 0] = shifted[lax.rem(item, tiles), starts[lax.div(item, tiles)]]
+        cond_ref[d // half_slots, d % half_slots, 0] = shifted[lax.rem(item, tiles), starts[lax.div(item, tiles)]]
 
     loads["mlp_in"].wait()
     loads["mlp_out"].wait()
-    await_bytes(noisy_in.at[pl.ds(0, slots - 1)], noisy_recv)
-    state = jnp.dot(
-        noisy_in[...].reshape(rows, channels), noise_w[...], preferred_element_type=jnp.float32
-    ).reshape(slots, ratio, window_len, channels)
-    state = (state + cond_ref[...]).reshape(slots * ratio, window_len, channels)
     step_row = lax.broadcasted_iota(jnp.int32, (window_len, channels), 0)
-    for layer in range(layers):
-        inverse = lax.rsqrt(jnp.mean(state * state, axis=-1, keepdims=True) + 1e-06)
-        plain = state * inverse
-        gain = gains[pl.ds(layer, 1), :] * 0.5
-        taps = tconv[layer]
-        before = jnp.where(step_row == 0, 0.0, taps[0:1] * gain)
-        here = gain + taps[1:2] * gain
-        behind = jnp.where(step_row == window_len - 1, 0.0, taps[2:3] * gain)
-        mixed = (
-            here[None] * plain
-            + before[None] * pltpu.roll(plain, 1, 1)
-            + behind[None] * pltpu.roll(plain, window_len - 1, 1)
-        )
-        mixed = mixed.reshape(rows, channels).astype(jnp.bfloat16)
-        half = jnp.dot(mixed, mlp_in[layer], preferred_element_type=jnp.float32)
-        hidden = (half + half * jnp.tanh(half)).astype(jnp.bfloat16)
-        state = state + jnp.dot(
-            hidden, mlp_out[layer], preferred_element_type=jnp.float32
-        ).reshape(slots * ratio, window_len, channels)
-    refined = state.reshape(rows, channels).astype(jnp.bfloat16)
-    video = jnp.dot(matrix, refined, preferred_element_type=jnp.float32) / denom
+    groups = half_slots * ratio
+    video = None
+    for group, chosen in enumerate((side, 1 - side)):
+        await_bytes(noisy_in.at[0, pl.ds(0, half_slots - 1 + group)], noisy_recv.at[group])
+        state = jnp.dot(
+            noisy_in[chosen].reshape(half_rows, channels), noise_w[...],
+            preferred_element_type=jnp.float32,
+        ).reshape(half_slots, ratio, window_len, channels)
+        state = (state + cond_ref[chosen]).reshape(groups, window_len, channels)
+        for layer in range(layers):
+            inverse = lax.rsqrt(jnp.mean(state * state, axis=-1, keepdims=True) + 1e-06)
+            plain = state * inverse
+            gain = gains[pl.ds(layer, 1), :] * 0.5
+            taps = tconv[layer]
+            before = jnp.where(step_row == 0, 0.0, taps[0:1] * gain)
+            here = gain + taps[1:2] * gain
+            behind = jnp.where(step_row == window_len - 1, 0.0, taps[2:3] * gain)
+            mixed = (
+                here[None] * plain
+                + before[None] * pltpu.roll(plain, 1, 1)
+                + behind[None] * pltpu.roll(plain, window_len - 1, 1)
+            )
+            mixed = mixed.reshape(half_rows, channels).astype(jnp.bfloat16)
+            half = jnp.dot(mixed, mlp_in[layer], preferred_element_type=jnp.float32)
+            hidden = (half + half * jnp.tanh(half)).astype(jnp.bfloat16)
+            state = state + jnp.dot(
+                hidden, mlp_out[layer], preferred_element_type=jnp.float32
+            ).reshape(groups, window_len, channels)
+        refined = state.reshape(half_rows, channels).astype(jnp.bfloat16)
+        term = jnp.dot(matrices[chosen], refined, preferred_element_type=jnp.float32)
+        video = term if video is None else video + term
+    video = video * scale
     video_out[...] = video.astype(jnp.bfloat16).reshape(slots, tiles * ratio, channels)
     for there in partners:
         send(video_out.at[there], out_ref.at[me], there, video_send, video_recv)
@@ -493,12 +511,13 @@
             pltpu.VMEM((slots + 2, tiles, channels), full),
             pltpu.VMEM((window_len * tile_pos, channels), full),
             pltpu.VMEM((slots, ratio * window_len, channels), half),
-            pltpu.VMEM((slots, ratio * window_len, channels), half),
+            pltpu.VMEM((2, slots // 2, ratio * window_len, channels), half),
             pltpu.VMEM((tiles * slots, channels), full),
             pltpu.VMEM((tiles, slots - window_len + 1, window_len, channels), full),
-            pltpu.VMEM((slots, 1, window_len, channels), full),
+            pltpu.VMEM((2, slots // 2, 1, window_len, channels), full),
             pltpu.VMEM((slots, tiles * ratio, channels), half),
-            dma((len(args),)), dma, dma, dma, dma, dma, dma, dma,
+            pltpu.VMEM((2, slots * tiles * ratio, rows // 2), half),
+            dma((len(args),)), dma, dma, dma, dma((2,)), dma, dma, dma,
         ],
         compiler_params=pltpu.CompilerParams(
             collective_id=0, has_side_effects=True, vmem_limit_bytes=60 * 1024 * 1024
@@ -524,7 +543,7 @@
     low_pos = lowres.shape[1] // tiles
     ratio = noisy.shape[2] // low_pos
     if (
-        low_pos == slots and tiles <= SUBLANES and noisy.shape[1] == SUBLANES
+        low_pos == slots and slots % 2 == 0 and tiles <= SUBLANES and noisy.shape[1] == SUBLANES
         and (tiles * ratio) % 16 == 0
     ):
         return split_on_device(*args)

time: 20.1 us -> 19.5 us (0.970)
  Pallas kernels: 19.9 us -> 19.3 us
    pallas_call x1, Pallas kernels: 18.3 us -> 17.8 us  [split_on_device(): pl.pallas_call(split_kernel, out_shape=jax.ShapeDtypeStruct((slots, tiles...]
where the time goes in v5:
time: 19.5 us; the launch traced here: 19.3 us
  Pallas kernels  19.3 us (99%)
    pallas_call x1, Pallas kernels, split_on_device(): pl.pallas_call(split_kernel, out_shape=jax.ShapeDtypeStruct((slots, tiles...  17.8 us
    pallas_call x1, Pallas kernels, split_on_device(): pl.pallas_call(functools.partial(order_kernel, tiles), out_shape=jax.Shap...  1.53 us

profile of v5, /device:TPU:0, one launch (start us, length us, event | category | flops | bytes accessed | tf_op | source)
XLA Modules:
  0.0 19.3 jit_solution(15185701669397443254)
XLA Ops:
  0.0 17.8 %shard_map.118.video_ref = bf16[16,16,128]{2,1,0:T(8,128)(2,1)} custom-call(bf16[4,16,128]{2,1,0:T(8,128)(2,1)} %bitcast.1, bf16[1,8,64,128]{3,2,1,0:T(8,128)(2,1)} %noisy_hbm.1, s32[4]{0:T(128)} %starts_hbm.1, s32[4,8]{1,0:T(4,128)} %blend_hbm.1, s32[16]{0:T(128)} %assign_hbm.1, bf16[3,128,128]{2,1,0:T(8,128)(2,1)} %base_w_hbm.1, ...), custom_call_target="tpu_custom_call" | custom-call | tf_op jit(solution)/shard_map/pallas_call | solution.py:492
  17.8 1.5 %shard_map.119 = bf16[1,256,128]{2,1,0:T(8,128)(2,1)} custom-call(bf16[16,16,128]{2,1,0:T(8,128)(2,1)} %shard_map.118.video_ref), custom_call_target="tpu_custom_call" | custom-call | tf_op jit(solution)/shard_map/pallas_call | solution.py:526

commit v6 on v5

--- a/solution.py
+++ b/solution.py
@@ -308,6 +308,8 @@
         ("mlp_out", mlp_out_hbm, mlp_out),
     )):
         loads[name] = pltpu.make_async_copy(source, target, load_sem.at[spot])
+    urgent = ("lowres", "noisy")
+    for name in urgent:
         loads[name].start()
 
     half_slots = slots // 2
@@ -325,6 +327,9 @@
         pl.semaphore_signal(
             barrier, inc=1, device_id={AXIS: there}, device_id_type=pl.DeviceIdType.MESH
         )
+    for name, load in loads.items():
+        if name not in urgent:
+            load.start()
 
     def send(source, target, there, send_sem, recv_sem):
         pltpu.make_async_remote_copy(
@@ -342,6 +347,10 @@
     for t in range(tiles):
         low_out[:, t, :] = lowres[t].astype(jnp.float32)
     low_in[me + 1] = low_out[me]
+
+    pl.semaphore_wait(barrier, slots - 1)
+    for there in partners:
+        send(low_out.at[there], low_in.at[me + 1], there, low_send, low_recv)
 
     loads["noisy"].wait()
     noisy_wide[...] = noisy[...].reshape(window_len * tile_pos, channels).astype(jnp.float32)
@@ -352,9 +361,6 @@
         noisy_out[j] = jnp.concatenate(picked, 0).astype(jnp.bfloat16)
     noisy_in[side, place] = noisy_out[me]
 
-    pl.semaphore_wait(barrier, slots - 1)
-    for there in partners:
-        send(low_out.at[there], low_in.at[me + 1], there, low_send, low_recv)
     for group, targets in enumerate((near, away)):
         for there in targets:
             send(
@@ -397,6 +403,16 @@
 
     for name in ("base_w", "cond_w", "noise_w", "gains", "tconv"):
         loads[name].wait()
+    step_row = lax.broadcasted_iota(jnp.int32, (window_len, channels), 0)
+    taps = []
+    for layer in range(layers):
+        gain = gains[pl.ds(layer, 1), :] * 0.5
+        tap = tconv[layer]
+        taps.append((
+            jnp.where(step_row == 0, 0.0, tap[0:1] * gain),
+            gain + tap[1:2] * gain,
+            jnp.where(step_row == window_len - 1, 0.0, tap[2:3] * gain),
+        ))
     await_bytes(low_in.at[pl.ds(0, slots - 1)], low_recv)
     total = None
     for k in range(3):
@@ -419,7 +435,6 @@
 
     loads["mlp_in"].wait()
     loads["mlp_out"].wait()
-    step_row = lax.broadcasted_iota(jnp.int32, (window_len, channels), 0)
     groups = half_slots * ratio
     video = None
     for group, chosen in enumerate((side, 1 - side)):
@@ -432,11 +447,7 @@
         for layer in range(layers):
             inverse = lax.rsqrt(jnp.mean(state * state, axis=-1, keepdims=True) + 1e-06)
             plain = state * inverse
-            gain = gains[pl.ds(layer, 1), :] * 0.5
-            taps = tconv[layer]
-            before = jnp.where(step_row == 0, 0.0, taps[0:1] * gain)
-            here = gain + taps[1:2] * gain
-            behind = jnp.where(step_row == window_len - 1, 0.0, taps[2:3] * gain)
+            before, here, behind = taps[layer]
             mixed = (
                 here[None] * plain
                 + before[None] * pltpu.roll(plain, 1, 1)

time: 19.5 us -> 19.5 us (level)
  no operation moved by 1% of the time
where the time goes in v6:
time: 19.5 us; the launch traced here: 19.3 us
  Pallas kernels  19.2 us (98%)
    pallas_call x1, Pallas kernels, split_on_device(): pl.pallas_call(split_kernel, out_shape=jax.ShapeDtypeStruct((slots, tiles...  17.7 us
    pallas_call x1, Pallas kernels, split_on_device(): pl.pallas_call(functools.partial(order_kernel, tiles), out_shape=jax.Shap...  1.53 us

profile of v6, /device:TPU:0, one launch (start us, length us, event | category | flops | bytes accessed | tf_op | source)
XLA Modules:
  0.0 19.3 jit_solution(1663231118568600490)
XLA Ops:
  0.0 17.7 %shard_map.118.video_ref = bf16[16,16,128]{2,1,0:T(8,128)(2,1)} custom-call(bf16[4,16,128]{2,1,0:T(8,128)(2,1)} %bitcast.1, bf16[1,8,64,128]{3,2,1,0:T(8,128)(2,1)} %noisy_hbm.1, s32[4]{0:T(128)} %starts_hbm.1, s32[4,8]{1,0:T(4,128)} %blend_hbm.1, s32[16]{0:T(128)} %assign_hbm.1, bf16[3,128,128]{2,1,0:T(8,128)(2,1)} %base_w_hbm.1, ...), custom_call_target="tpu_custom_call" | custom-call | tf_op jit(solution)/shard_map/pallas_call | solution.py:503
  17.7 1.5 %shard_map.119 = bf16[1,256,128]{2,1,0:T(8,128)(2,1)} custom-call(bf16[16,16,128]{2,1,0:T(8,128)(2,1)} %shard_map.118.video_ref), custom_call_target="tpu_custom_call" | custom-call | tf_op jit(solution)/shard_map/pallas_call | solution.py:537

commit v7 on v6

--- a/solution.py
+++ b/solution.py
@@ -348,10 +348,6 @@
         low_out[:, t, :] = lowres[t].astype(jnp.float32)
     low_in[me + 1] = low_out[me]
 
-    pl.semaphore_wait(barrier, slots - 1)
-    for there in partners:
-        send(low_out.at[there], low_in.at[me + 1], there, low_send, low_recv)
-
     loads["noisy"].wait()
     noisy_wide[...] = noisy[...].reshape(window_len * tile_pos, channels).astype(jnp.float32)
     for j in range(slots):
@@ -360,6 +356,10 @@
         ]
         noisy_out[j] = jnp.concatenate(picked, 0).astype(jnp.bfloat16)
     noisy_in[side, place] = noisy_out[me]
+
+    pl.semaphore_wait(barrier, slots - 1)
+    for there in partners:
+        send(low_out.at[there], low_in.at[me + 1], there, low_send, low_recv)
 
     for group, targets in enumerate((near, away)):
         for there in targets:

time: 19.5 us -> 19.5 us (level)
  no operation moved by 1% of the time
where the time goes in v7:
time: 19.5 us; the launch traced here: 19.2 us
  Pallas kernels  19.2 us (98%)
    pallas_call x1, Pallas kernels, split_on_device(): pl.pallas_call(split_kernel, out_shape=jax.ShapeDtypeStruct((slots, tiles...  17.7 us
    pallas_call x1, Pallas kernels, split_on_device(): pl.pallas_call(functools.partial(order_kernel, tiles), out_shape=jax.Shap...  1.53 us

profile of v7, /device:TPU:0, one launch (start us, length us, event | category | flops | bytes accessed | tf_op | source)
XLA Modules:
  0.0 19.2 jit_solution(11667012187201953306)
XLA Ops:
  0.0 17.7 %shard_map.118.video_ref = bf16[16,16,128]{2,1,0:T(8,128)(2,1)} custom-call(bf16[4,16,128]{2,1,0:T(8,128)(2,1)} %bitcast.1, bf16[1,8,64,128]{3,2,1,0:T(8,128)(2,1)} %noisy_hbm.1, s32[4]{0:T(128)} %starts_hbm.1, s32[4,8]{1,0:T(4,128)} %blend_hbm.1, s32[16]{0:T(128)} %assign_hbm.1, bf16[3,128,128]{2,1,0:T(8,128)(2,1)} %base_w_hbm.1, ...), custom_call_target="tpu_custom_call" | custom-call | tf_op jit(solution)/shard_map/pallas_call | solution.py:503
  17.7 1.5 %shard_map.119 = bf16[1,256,128]{2,1,0:T(8,128)(2,1)} custom-call(bf16[16,16,128]{2,1,0:T(8,128)(2,1)} %shard_map.118.video_ref), custom_call_target="tpu_custom_call" | custom-call | tf_op jit(solution)/shard_map/pallas_call | solution.py:537

commit v8 on v7

--- a/solution.py
+++ b/solution.py
@@ -502,9 +502,9 @@
     dma = pltpu.SemaphoreType.DMA
     video = pl.pallas_call(
         split_kernel,
-        out_shape=jax.ShapeDtypeStruct((slots, tiles * ratio, channels), half),
+        out_shape=pltpu.VMEM((slots, tiles * ratio, channels), half),
         in_specs=[pl.BlockSpec(memory_space=pl.ANY)] * len(args),
-        out_specs=pl.BlockSpec(memory_space=pl.ANY),
+        out_specs=pl.BlockSpec(memory_space=pltpu.VMEM),
         scratch_shapes=[
             pltpu.VMEM((tiles, low_pos, channels), half),
             pltpu.VMEM(noisy.shape[1:], half),
@@ -543,7 +543,7 @@
             pltpu.VMEM((tiles * tile_pos, channels), full),
             pltpu.VMEM((tiles * tile_pos, channels), full),
         ],
-        compiler_params=pltpu.CompilerParams(vmem_limit_bytes=60 * 1024 * 1024),
+        compiler_params=pltpu.CompilerParams(vmem_limit_bytes=16 * 1024 * 1024),
     )(video)
 
 

time: 19.5 us -> 18.5 us (0.949)
  Pallas kernels: 19.2 us -> 18.3 us
    pallas_call x1, Pallas kernels: 1.53 us -> 0.69 us  [split_on_device(): pl.pallas_call(functools.partial(order_kernel, tiles), out_shape=jax.Shap...]
where the time goes in v8:
time: 18.5 us; the launch traced here: 18.3 us
  Pallas kernels  18.3 us (99%)
    pallas_call x1, Pallas kernels, split_on_device(): pl.pallas_call(split_kernel, out_shape=pltpu.VMEM((slots, tiles * ratio,...  17.6 us
    pallas_call x1, Pallas kernels, split_on_device(): pl.pallas_call(functools.partial(order_kernel, tiles), out_shape=jax.Shap...  0.69 us

profile of v8, /device:TPU:0, one launch (start us, length us, event | category | flops | bytes accessed | tf_op | source)
XLA Modules:
  0.0 18.3 jit_solution(5574761659285526381)
XLA Ops:
  0.0 17.6 %shard_map.118.video_ref = bf16[16,16,128]{2,1,0:T(8,128)(2,1)S(1)} custom-call(bf16[4,16,128]{2,1,0:T(8,128)(2,1)} %bitcast.1, bf16[1,8,64,128]{3,2,1,0:T(8,128)(2,1)} %noisy_hbm.1, s32[4]{0:T(128)} %starts_hbm.1, s32[4,8]{1,0:T(4,128)} %blend_hbm.1, s32[16]{0:T(128)} %assign_hbm.1, bf16[3,128,128]{2,1,0:T(8,128)(2,1)} %base_w_hbm.1, ...), custom_call_target="tpu_custom_call" | custom-call | tf_op jit(solution)/shard_map/pallas_call | solution.py:503
  17.6 0.7 %shard_map.119 = bf16[1,256,128]{2,1,0:T(8,128)(2,1)} custom-call(bf16[16,16,128]{2,1,0:T(8,128)(2,1)S(1)} %shard_map.118.video_ref), custom_call_target="tpu_custom_call" | custom-call | tf_op jit(solution)/shard_map/pallas_call | solution.py:537
